TPU v7x, 32 devices: a whole 2x2x4 slice. The times are simulated.
32 devices in a mesh: dp: 4 (over y, x), mp: 8 (over z, core).
Axes of the slice: x: 2, y: 2, z: 4, core: 2. Of those that a mesh axis runs over, the one named last changes fastest.
Arguments:
- activations: bfloat16 [4096, 2048], P('dp', 'mp'), may hold values from -6 to 6
- out_grad: bfloat16 [4096, 8192], P('dp'), may hold values from -0.8984375 to 0.8984375
- old_weight: bfloat16 [8, 256, 8192], P('mp', 'dp'), may hold values from -0.125 to 0.125
- old_first: float32 [8, 256, 8192], P('mp', 'dp'), may hold values from -6 to 6
- old_second: float32 [8, 256, 8192], P('mp', 'dp'), may hold values from 0.25 to 4
- step: int32 [1], replicated, may hold values from 1 to 31
- next_input: bfloat16 [4096, 2048], P('dp', 'mp'), may hold values from -6 to 6
Outputs:
- new_weight: bfloat16 [8, 344, 8192], P('mp', 'dp')
- new_first: float32 [8, 344, 8192], P('mp', 'dp')
- new_second: float32 [8, 344, 8192], P('mp', 'dp')
- output: bfloat16 [4096, 8192], P('dp', 'mp')
Inputs may be any that keep to these rules, and one draw needn't show every extreme that they name: `step`: the number of Adam steps taken, this one included.
All inputs are finite; a program needn't handle non-finite values.
Results may differ from a plain program's by a relative error of at most 0.0049.
Values may be sent and summed in bfloat16 or wider, within the bound.
A program may use at most 192 MiB of HBM per device.

v0:
```python
import jax
import jax.numpy as jnp
from jax import lax
from jax.sharding import PartitionSpec as P


def from_behind(block, axis, distance):
    devices = range(lax.axis_size(axis))
    route = [(i - distance, i) for i in devices if i - distance in devices]
    return lax.ppermute(block, axis, route)


def body(activations, out_grad, old_weight, old_first, old_second, step, next_input):
    owners = lax.axis_size("dp")
    owner = lax.axis_index("dp")
    old_rows = old_weight.shape[1]
    width = old_weight.shape[2]
    held_rows = old_rows * owners
    shard_rows = (held_rows + owners - 2) // (owners - 1)
    padded_rows = owners * shard_rows
    tok_rows = activations.shape[0]
    moments = jnp.stack([old_first[0], old_second[0]])
    weight_next = from_behind(old_weight[0], "dp", -1)
    moment_next = from_behind(moments, "dp", -1)
    weight_rows = jnp.concatenate(
        [old_weight[0], weight_next, jnp.zeros((shard_rows, width), jnp.bfloat16)], 0
    )
    moment_rows = jnp.concatenate(
        [moments, moment_next, jnp.zeros((2, shard_rows, width), jnp.float32)], 1
    )
    begin = owner * (shard_rows - old_rows)
    weight_mine = lax.dynamic_slice_in_dim(weight_rows, begin, shard_rows, 0)
    moment_mine = lax.dynamic_slice_in_dim(moment_rows, begin, shard_rows, 1)
    row_index = owner * shard_rows + lax.broadcasted_iota(jnp.int32, (shard_rows, 1), 0)
    valid = row_index < held_rows
    feat_pad = jnp.concatenate(
        [activations, jnp.zeros((tok_rows, padded_rows - held_rows), jnp.bfloat16)], 1
    )
    grad = lax.psum_scatter(
        lax.dot_general(
            feat_pad, out_grad, (((0,), (0,)), ((), ())), preferred_element_type=jnp.float32
        ),
        "dp",
        scatter_dimension=0,
        tiled=True,
    )
    step_float = step[0].astype(jnp.float32)
    first_fix = 1.0 - jnp.power(jnp.float32(0.9), step_float)
    second_fix = 1.0 - jnp.power(jnp.float32(0.95), step_float)
    new_first = 0.9 * moment_mine[0] + 0.1 * grad
    new_second = 0.95 * moment_mine[1] + 0.05 * grad * grad
    safe_second = jnp.where(valid, new_second, jnp.float32(1.0))
    update = new_first / first_fix / (jnp.sqrt(safe_second / second_fix) + 1e-08)
    update = jnp.where(valid, update, jnp.float32(0.0))
    new_weight = (weight_mine.astype(jnp.float32) - 0.01 * update).astype(jnp.bfloat16)
    weight_all_new = lax.all_gather(new_weight, "dp", axis=0, tiled=True)[:held_rows]
    weight_cols = lax.all_to_all(weight_all_new, "mp", split_axis=1, concat_axis=0, tiled=True)
    input_all = lax.all_gather(next_input, "mp", axis=1, tiled=True)
    output = jnp.dot(input_all, weight_cols, preferred_element_type=jnp.float32).astype(
        jnp.bfloat16
    )
    return (new_weight[None], new_first[None], new_second[None], output)


def solution(mesh):
    return jax.shard_map(
        body,
        mesh=mesh,
        in_specs=(
            P("dp", "mp"),
            P("dp", None),
            P("mp", "dp", None),
            P("mp", "dp", None),
            P("mp", "dp", None),
            P(),
            P("dp", "mp"),
        ),
        out_specs=(P("mp", "dp", None), P("mp", "dp", None), P("mp", "dp", None), P("dp", "mp")),
        check_vma=False,
    )
```

profile of v0, /device:TPU:0, one launch (start us, length us, event | category | flops | bytes accessed | tf_op | source)
XLA Modules:
  0.0 492.6 jit_solution(16472965787498967166)
XLA Ops:
  7.2 0.0 copy-start.1
  7.2 0.0 all-gather.6.cloned.1.call-start
  7.2 3.2 constant_dynamic-update-slice_fusion.1
  10.4 0.0 copy-done.1
  10.4 0.0 copy-start.3
  10.4 1.5 constant_dynamic-update-slice_fusion
  11.9 1.3 collective-permute-start.1
  13.2 0.0 copy-done.3
  13.2 12.2 %fusion.10 = f32[344,8192]{1,0:T(8,128)} fusion(bf16[1024,8192]{1,0:T(8,128)(2,1)} %param.8, bf16[1024,256]{1,0:T(8,128)(2,1)S(1)} %copy-done.3), kind=kOutput, calls=%fused_computation.19 | convolution fusion | flops 5771362304 | bytes 28573696 | tf_op jit(solution)/shard_map/dot_general | solution.py:40
  25.4 0.0 copy-start.4
  25.4 190.4 %fusion = f32[96,8192]{1,0:T(8,128)S(1)} fusion(f32[344,8192]{1,0:T(8,128)} %fusion.10), kind=kCustom, calls=%all-reduce-scatter | all-reduce-scatter fusion | flops 3145729 | bytes 14418432
  215.8 1.0 slice.15
  216.8 4.7 collective-permute-start.2
  221.5 1.3 collective-permute-start
  223.5 0.0 copy-done.4
  223.5 0.6 dynamic-slice.6
  224.8 0.1 pad_dynamic-slice_fusion.4
  224.9 0.1 pad_dynamic-slice_fusion.5
  225.0 17.6 %collective-permute-done.2 = f32[30,8192]{1,0:T(8,128)} collective-permute-done((f32[30,8192]{1,0:T(8,128)}, f32[30,8192]{1,0:T(8,128)}, u32[]{:S(2)}, u32[]{:S(2)}) %collective-permute-start.2) | collective-permute-done | bytes 983072
  242.6 12.3 %concatenate.12 = f32[126,8192]{1,0:T(8,128)} concatenate(f32[30,8192]{1,0:T(8,128)} %collective-permute-done.2, f32[96,8192]{1,0:T(8,128)S(1)} %fusion), dimensions={0} | concatenate | bytes 8257536
  254.9 0.0 copy-start
  254.9 0.0 copy-start.2
  254.9 0.0 collective-permute-done.1
  254.9 4.4 fusion.2
  259.3 7.7 %collective-permute-done = bf16[64,8192]{1,0:T(8,128)(2,1)} collective-permute-done((bf16[64,8192]{1,0:T(8,128)(2,1)}, bf16[64,8192]{1,0:T(8,128)(2,1)}, u32[]{:S(2)}, u32[]{:S(2)}) %collective-permute-start) | collective-permute-done | bytes 1048608 | tf_op jit(solution)/shard_map/ppermute | solution.py:10
  267.0 0.0 copy-done
  267.0 0.0 copy-done.2
  267.0 5.9 %fusion.13 = (f32[1,86,8192]{2,1,0:T(8,128)S(1)}, f32[1,86,8192]{2,1,0:T(8,128)}, bf16[1,86,8192]{2,1,0:T(8,128)(2,1)}) fusion(f32[126,8192]{1,0:T(8,128)S(1)} %copy-done, u32[]{:S(6)} %subtract, f32[2,86,8192]{2,1,0:T(8,128)S(1)} %fusion.2, f32[]{:T(128)} %bitcast.4, f32[]{:T(128)} %bitcast.2, pred[86]{0:T(512)(128)(4,1)S(1)} %add_compare_fusion, ...), kind=kLoop, calls=%fused_computation.22 | loop fusion | flops 15499264 | bytes 17596690 | tf_op jit(solution)/shard_map/broadcast_in_dim | solution.py:62
  272.9 0.0 all-gather.6.cloned.1.call-update
  272.9 0.0 all-gather.4.cloned.1.call-start
  272.9 0.7 all-gather.4.cloned.1.call-update
  273.6 64.6 %all-gather.6.cloned.1.call-done = bf16[4,86,8192]{2,1,0:T(8,128)(2,1)} async-done(((bf16[1,86,8192]{2,1,0:T(8,128)(2,1)}), bf16[4,86,8192]{2,1,0:T(8,128)(2,1)}) %all-gather.6.cloned.1.call-update) | async-done | bytes 5636112 | tf_op jit(solution)/shard_map/all_gather | solution.py:56
  338.2 6.9 %reshape.32 = bf16[344,8192]{1,0:T(8,128)(2,1)} reshape(bf16[4,86,8192]{2,1,0:T(8,128)(2,1)} %all-gather.6.cloned.1.call-done) | data formatting | bytes 11272192
  345.1 0.0 slice-start
  345.1 2.4 slice-done
  347.5 2.4 copy.24
  349.9 4.7 all-to-all-start
  354.7 6.3 %copy.19 = f32[1,86,8192]{2,0,1:T(1,128)} copy(f32[1,86,8192]{2,1,0:T(8,128)} %get-tuple-element.17) | data formatting | bytes 5636096
  361.0 4.5 copy.20
  365.4 57.2 %all-gather.4.cloned.1.call-done = bf16[1024,2048]{1,0:T(8,128)(2,1)} async-done(((bf16[1024,256]{1,0:T(8,128)(2,1)}), bf16[1024,2048]{1,0:T(8,128)(2,1)}) %all-gather.4.cloned.1.call-update) | async-done | bytes 4194320 | tf_op jit(solution)/shard_map/all_gather | solution.py:58
  422.7 52.5 %all-to-all-done = bf16[256,8,1024]{2,0,1:T(8,128)(2,1)} async-done(((bf16[256,8,1024]{2,0,1:T(8,128)(2,1)}), bf16[256,8,1024]{2,0,1:T(8,128)(2,1)}, u32[]{:S(2)}, u32[]{:S(2)}) %all-to-all-start) | async-done | bytes 4194336 | tf_op jit(solution)/shard_map/all_to_all | solution.py:57
  475.2 8.0 %convert_bitcast_fusion = bf16[1024,1024]{0,1:T(8,128)(2,1)S(1)} fusion(bf16[2048,1024]{1,0:T(8,128)(2,1)} %bitcast.9, bf16[1024,2048]{1,0:T(8,128)(2,1)} %all-gather.4.cloned.1.call-done), kind=kOutput, calls=%fused_computation.15 | convolution fusion | flops 4296015872 | bytes 10485760 | tf_op jit(solution)/shard_map/dot_general | solution.py:59
  483.2 2.6 copy.21
  (3 shorter events, 0.0 us)
Async XLA Ops:
  7.2 3.2 copy-start.1
  7.2 331.0 %all-gather.6.cloned.1.call-start = ((), (), s32[]{:S(2)}) async-start(), calls=%async_computation.2 | async-start | bytes 7208960 | tf_op jit(solution)/shard_map/all_gather | solution.py:56
  10.4 2.8 copy-start.3
  11.9 243.0 %collective-permute-start.1 = (f32[2,64,8192]{2,1,0:T(8,128)}, f32[2,64,8192]{2,1,0:T(8,128)}, u32[]{:S(2)}, u32[]{:S(2)}) collective-permute-start(f32[2,64,8192]{2,1,0:T(8,128)} %constant_dynamic-update-slice_fusion), channel_id=1, source_target_pairs={{8,0},{16,8},{24,16},{9,1},{17,9},{25,17},{10,2},{18,10},{26,18},{... | collective-permute-start | bytes 12582920 | tf_op jit(solution)/shard_map/ppermute | solution.py:10
  25.4 198.2 %copy-start.4 = (u32[32]{0:T(128)S(1)}, u32[32]{0:T(128)}, u32[]{:S(2)}) copy-start(u32[32]{0:T(128)} %constant.51) | copy-start | bytes 388
  216.8 25.7 %collective-permute-start.2 = (f32[30,8192]{1,0:T(8,128)}, f32[30,8192]{1,0:T(8,128)}, u32[]{:S(2)}, u32[]{:S(2)}) collective-permute-start(f32[30,8192]{1,0:T(8,128)} %slice.15), channel_id=1, source_target_pairs={{0,8},{8,16},{16,24},{1,9},{9,17},{17,25},{2,10},{10,18},{18,26},{... | collective-permute-start | bytes 2949128
  221.5 45.5 %collective-permute-start = (bf16[64,8192]{1,0:T(8,128)(2,1)}, bf16[64,8192]{1,0:T(8,128)(2,1)}, u32[]{:S(2)}, u32[]{:S(2)}) collective-permute-start(bf16[64,8192]{1,0:T(8,128)(2,1)} %bitcast.42), channel_id=1, source_target_pairs={{8,0},{16,8},{24,16},{9,1},{17,9},{25,17},{10,2},{18,10},{26,18},{... | collective-permute-start | bytes 3145736 | tf_op jit(solution)/shard_map/ppermute | solution.py:10
  254.9 12.1 %copy-start = (f32[126,8192]{1,0:T(8,128)S(1)}, f32[126,8192]{1,0:T(8,128)}, u32[]{:S(2)}) copy-start(f32[126,8192]{1,0:T(8,128)} %concatenate.12) | copy-start | bytes 12386308
  254.9 12.1 %copy-start.2 = (bf16[1,64,8192]{2,1,0:T(8,128)(2,1)S(1)}, bf16[1,64,8192]{2,1,0:T(8,128)(2,1)}, u32[]{:S(2)}) copy-start(bf16[1,64,8192]{2,1,0:T(8,128)(2,1)} %param.9) | copy-start | bytes 3145732
  272.9 149.8 %all-gather.4.cloned.1.call-start = ((), (), s32[]{:S(2)}) async-start(), calls=%async_computation.1 | async-start | bytes 4718592 | tf_op jit(solution)/shard_map/all_gather | solution.py:58
  345.1 2.4 slice-start
  349.9 125.3 %all-to-all-start = ((bf16[256,8,1024]{2,0,1:T(8,128)(2,1)}), bf16[256,8,1024]{2,0,1:T(8,128)(2,1)}, u32[]{:S(2)}, u32[]{:S(2)}) async-start(bf16[256,8,1024]{2,0,1:T(8,128)(2,1)} %bitcast.41), calls=%async_computation | async-start | bytes 8388608 | tf_op jit(solution)/shard_map/all_to_all | solution.py:57
Sparse Core Ops, SparseCore 0:
  273.0 65.1 all-gather.5
  339.8 82.8 all-gather.3
where the time goes:
time: 494 us; the launch traced here: 493 us
  waiting for transfers between devices  200 us (40%)
  blocking collectives  190 us (38%)
  local copies, waits for them, and re-layouts  43.9 us (9%)
  matrix products  20.2 us (4%)
  between operations  15.5 us (3%)
  starting transfers between devices  12 us (2%)
  other arithmetic  10.3 us (2%)
    unnamed x1, blocking collectives  190 us
    all_gather x1, waiting for transfers between devices, body(): lax.all_gather(new_weight, 'dp', axis=0, tiled=True)[:held_rows]  64.6 us
    all_gather x1, waiting for transfers between devices, body(): input_all = lax.all_gather(next_input, 'mp', axis=1, tiled=True)  57.2 us
    all_to_all x1, waiting for transfers between devices, body(): lax.all_to_all(weight_all_new, 'mp', split_axis=1, concat_axis=0, tiled=T...  52.5 us
    unnamed x18, local copies, waits for them, and re-layouts  37.4 us
    unnamed x3, waiting for transfers between devices  18.3 us
    dot_general x1, matrix products, body(): lax.dot_general(feat_pad, out_grad, (((0,), (0,)), ((), ())), preferred_e...  12.2 us
  transfers between devices with their start and end apart: 6, of which 5 were waited for; matrix products, arithmetic and copies ran while one was open for 49% of the time, Pallas kernels for 0%

commit v1 on v0

v1 whole, which is shorter than its diff:
```python
import jax
import jax.numpy as jnp
from jax import lax
from jax.sharding import PartitionSpec as P


def partner(i, k, n):
    return i ^ k if n & (n - 1) == 0 else (i + k) % n


def exchange(block, axis, k):
    n = lax.axis_size(axis)
    return lax.ppermute(block, axis, [(i, partner(i, k, n)) for i in range(n)])


def target(k, n, axis):
    me = lax.axis_index(axis)
    return me ^ k if n & (n - 1) == 0 else lax.rem(me + k, n)


def to_front(block, axis):
    n = lax.axis_size(axis)
    return lax.ppermute(block, axis, [(i, i - 1) for i in range(1, n)])


def body(activations, out_grad, old_weight, old_first, old_second, step, next_input):
    owners = lax.axis_size("dp")
    owner = lax.axis_index("dp")
    old_rows = old_weight.shape[1]
    width = old_weight.shape[2]
    held_rows = old_rows * owners
    shard_rows = (held_rows + owners - 2) // (owners - 1)
    input_all = lax.all_gather(next_input, "mp", axis=1, tiled=True)

    part = lax.dot_general(
        activations, out_grad, (((0,), (0,)), ((), ())), preferred_element_type=jnp.float32
    ).astype(jnp.bfloat16)
    part = part.reshape(owners, old_rows, width)
    grad = lax.dynamic_index_in_dim(part, owner, 0, keepdims=False).astype(jnp.float32)
    for k in range(1, owners):
        away = lax.dynamic_index_in_dim(part, target(k, owners, "dp"), 0, keepdims=False)
        grad = grad + exchange(away, "dp", k).astype(jnp.float32)

    step_float = step[0].astype(jnp.float32)
    first_fix = 1.0 - jnp.power(jnp.float32(0.9), step_float)
    second_fix = 1.0 - jnp.power(jnp.float32(0.95), step_float)
    new_first = 0.9 * old_first[0] + 0.1 * grad
    new_second = 0.95 * old_second[0] + 0.05 * grad * grad
    update = new_first / first_fix / (jnp.sqrt(new_second / second_fix) + 1e-08)
    new_weight = (old_weight[0].astype(jnp.float32) - 0.01 * update).astype(jnp.bfloat16)

    weight_part = lax.all_to_all(new_weight, "mp", split_axis=1, concat_axis=0, tiled=True)
    heads = lax.axis_size("mp")
    weight_part = weight_part.reshape(heads, old_rows, -1)
    weight_cols = lax.all_gather(weight_part, "dp", axis=1, tiled=True)
    weight_cols = weight_cols.reshape(heads * held_rows, -1)

    begin = owner * (shard_rows - old_rows)

    def mine(block):
        behind = to_front(block.astype(jnp.bfloat16), "dp").astype(block.dtype)
        rows = jnp.concatenate([block, behind, jnp.zeros((shard_rows, width), block.dtype)], 0)
        return lax.dynamic_slice_in_dim(rows, begin, shard_rows, 0)[None]

    outs = (mine(new_weight), mine(new_first), mine(new_second))
    output = jnp.dot(input_all, weight_cols, preferred_element_type=jnp.float32).astype(
        jnp.bfloat16
    )
    return (*outs, output)


def solution(mesh):
    return jax.shard_map(
        body,
        mesh=mesh,
        in_specs=(
            P("dp", "mp"),
            P("dp", None),
            P("mp", "dp", None),
            P("mp", "dp", None),
            P("mp", "dp", None),
            P(),
            P("dp", "mp"),
        ),
        out_specs=(P("mp", "dp", None), P("mp", "dp", None), P("mp", "dp", None), P("dp", "mp")),
        check_vma=False,
    )
```

time: 494 us -> 293 us (0.59)
  blocking collectives: 190 us -> 31.3 us
  waiting for transfers between devices: 200 us -> 175 us
  local copies, waits for them, and re-layouts: 43.9 us -> 27.4 us
  other arithmetic: 10.3 us -> 17 us
    unnamed x1 -> x0, blocking collectives: 190 us -> none
    ppermute x2 -> x6, waiting for transfers between devices: 7.66 us -> 106 us  [the longest x3 60.5 us: to_front(): return lax.ppermute(block, axis, [(i, i - 1) for i in range(1, n)])]
    all_to_all x1 -> x0, waiting for transfers between devices: 52.5 us -> none  [body(): lax.all_to_all(weight_all_new, 'mp', split_axis=1, concat_axis=0, tiled=T...]
    all_gather x1, waiting for transfers between devices: 64.6 us -> 25.5 us  [body(): weight_cols = lax.all_gather(weight_part, 'dp', axis=1, tiled=True)]
    unnamed x18 -> x21, local copies, waits for them, and re-layouts: 37.4 us -> 5.95 us
    all_to_all x0 -> x1, blocking collectives: none -> 31.3 us  [body(): lax.all_to_all(new_weight, 'mp', split_axis=1, concat_axis=0, tiled=True)]
    unnamed x3 -> x2, waiting for transfers between devices: 18.3 us -> 0.71 us
    all_gather x1, waiting for transfers between devices: 57.2 us -> 42.9 us  [body(): input_all = lax.all_gather(next_input, 'mp', axis=1, tiled=True)]
  transfers between devices with their start and end apart: 6 -> 8, of which waited for: 5 -> 7; matrix products, arithmetic and copies ran while one was open for 49% -> 10% of each run, Pallas kernels for 0% -> 0%
where the time goes in v1:
time: 293 us
  waiting for transfers between devices  175 us (60%)
  blocking collectives  31.3 us (11%)
  local copies, waits for them, and re-layouts  27.4 us (9%)
  matrix products  19 us (6%)
  other arithmetic  17 us (6%)
  between operations  14.9 us (5%)
  starting transfers between devices  8.58 us (3%)
    ppermute x3, waiting for transfers between devices, to_front(): return lax.ppermute(block, axis, [(i, i - 1) for i in range(1, n)])  60.5 us
    ppermute x3, waiting for transfers between devices, exchange(): return lax.ppermute(block, axis, [(i, partner(i, k, n)) for i in range(n)])  45 us
    all_gather x1, waiting for transfers between devices, body(): input_all = lax.all_gather(next_input, 'mp', axis=1, tiled=True)  42.9 us
    all_to_all x1, blocking collectives, body(): lax.all_to_all(new_weight, 'mp', split_axis=1, concat_axis=0, tiled=True)  31.3 us
    all_gather x1, waiting for transfers between devices, body(): weight_cols = lax.all_gather(weight_part, 'dp', axis=1, tiled=True)  25.5 us
    broadcast_in_dim x2, local copies, waits for them, and re-layouts, mine(): return lax.dynamic_slice_in_dim(rows, begin, shard_rows, 0)[None]  11.4 us
    dot_general x1, matrix products, body(): lax.dot_general(activations, out_grad, (((0,), (0,)), ((), ())), preferre...  10.7 us
    convert_element_type x3, other arithmetic, mine(): behind = to_front(block.astype(jnp.bfloat16), 'dp').astype(block.dtype)  8.57 us
  transfers between devices with their start and end apart: 8, of which 7 were waited for; matrix products, arithmetic and copies ran while one was open for 10% of the time, Pallas kernels for 0%

profile of v1, /device:TPU:0, one launch (start us, length us, event | category | flops | bytes accessed | tf_op | source)
XLA Modules:
  0.0 292.9 jit_solution(17170010049314651664)
XLA Ops:
  7.2 0.0 copy-start
  7.2 0.0 all-gather.3.cloned.1.call-start
  7.2 1.0 copy-done
  8.2 10.7 %convolution_convert_fusion = bf16[256,8192]{1,0:T(8,128)(2,1)S(1)} fusion(bf16[1024,256]{1,0:T(8,128)(2,1)S(1)} %copy-done, bf16[1024,8192]{1,0:T(8,128)(2,1)} %param.8), kind=kOutput, calls=%fused_computation | convolution fusion | flops 4297064448 | bytes 21495808 | tf_op jit(solution)/shard_map/dot_general | solution.py:35
  19.0 0.0 copy-start.4
  19.0 1.8 dynamic-slice_bitcast_fusion.2
  20.7 1.2 copy-done.4
  21.9 2.9 %collective-permute-start = (bf16[64,8192]{1,0:T(8,128)(2,1)}, bf16[64,8192]{1,0:T(8,128)(2,1)S(1)}, u32[]{:S(2)}, u32[]{:S(2)}) collective-permute-start(bf16[64,8192]{1,0:T(8,128)(2,1)} %get-tuple-element.26), channel_id=1, source_target_pairs={{0,8},{8,0},{16,24},{24,16},{1,9},{9,1},{17,25},{25,17},{2,10},{10... | collective-permute-start | bytes 3145736 | tf_op jit(solution)/shard_map/ppermute | solution.py:13
  24.8 1.5 collective-permute-start.1
  26.4 0.0 collective-permute-start.2
  27.1 0.0 copy-start.9
  27.1 21.9 %collective-permute-done = bf16[64,8192]{1,0:T(8,128)(2,1)S(1)} collective-permute-done((bf16[64,8192]{1,0:T(8,128)(2,1)}, bf16[64,8192]{1,0:T(8,128)(2,1)S(1)}, u32[]{:S(2)}, u32[]{:S(2)}) %collective-permute-start) | collective-permute-done | bytes 1048608 | tf_op jit(solution)/shard_map/ppermute | solution.py:13
  49.0 23.1 %collective-permute-done.1 = bf16[64,8192]{1,0:T(8,128)(2,1)S(1)} collective-permute-done((bf16[64,8192]{1,0:T(8,128)(2,1)}, bf16[64,8192]{1,0:T(8,128)(2,1)S(1)}, u32[]{:S(2)}, u32[]{:S(2)}) %collective-permute-start.1) | collective-permute-done | bytes 1048608 | tf_op jit(solution)/shard_map/ppermute | solution.py:13
  72.1 0.0 copy-done.7
  72.2 1.0 copy-done.8
  73.1 0.0 collective-permute-done.2
  73.1 5.9 %fusion.11 = (bf16[64,8192]{1,0:T(8,128)(2,1)}, f32[64,8192]{1,0:T(8,128)S(1)}, bf16[64,8192]{1,0:T(8,128)(2,1)}, f32[64,8192]{1,0:T(8,128)S(1)}) fusion(bf16[64,8192]{1,0:T(8,128)(2,1)} %collective-permute-done.2, bf16[64,8192]{1,0:T(8,128)(2,1)} %copy-done.8, bf16[64,8192]{1,0:T(8,128)(2,1)} %copy-done.7, bf16[4,64,8192]{2,1,0:T(8,128)(2,1)} %bitcast.42, ...), kind=kLoop, calls=%fused_computation.29 | loop fusion | flops 8388608 | bytes 14680068 | tf_op jit(solution)/shard_map/convert_element_type | solution.py:61
  79.0 0.0 copy-done.9
  79.0 1.1 fusion.7
  80.1 0.2 copy-done.2
  80.3 0.1 copy.21
  80.4 31.3 %all_to_all.16 = bf16[64,8,1024]{2,0,1:T(8,128)(2,1)S(1)} all-to-all(bf16[64,8,1024]{2,0,1:T(8,128)(2,1)S(1)} %bitcast.46), channel_id=1, replica_groups=mesh['dp'=4,'mp'=8] {'mp'}, dimensions={1} | all-to-all | bytes 2097152 | tf_op jit(solution)/shard_map/all_to_all | solution.py:52
  111.7 0.0 copy-done.6
  111.7 1.5 copy.16
  113.2 0.0 all-gather.3.cloned.1.call-update
  113.2 0.0 all-gather.5.cloned.1.call-start
  113.3 0.7 all-gather.5.cloned.1.call-update
  114.0 1.3 collective-permute-start.4
  115.3 1.3 collective-permute-start.5
  116.6 0.1 pad_dynamic-slice_fusion.6
  116.7 0.1 pad_dynamic-slice_fusion.7
  116.8 1.5 collective-permute-start.3
  118.2 35.3 %collective-permute-done.4 = bf16[64,8192]{1,0:T(8,128)(2,1)} collective-permute-done((bf16[64,8192]{1,0:T(8,128)(2,1)}, bf16[64,8192]{1,0:T(8,128)(2,1)}, u32[]{:S(2)}, u32[]{:S(2)}) %collective-permute-start.4) | collective-permute-done | bytes 1048608 | tf_op jit(solution)/shard_map/ppermute | solution.py:23
  153.5 1.4 convert_element_type.60
  154.9 0.0 copy-start.3
  154.9 21.1 %collective-permute-done.5 = bf16[64,8192]{1,0:T(8,128)(2,1)} collective-permute-done((bf16[64,8192]{1,0:T(8,128)(2,1)}, bf16[64,8192]{1,0:T(8,128)(2,1)}, u32[]{:S(2)}, u32[]{:S(2)}) %collective-permute-start.5) | collective-permute-done | bytes 1048608 | tf_op jit(solution)/shard_map/ppermute | solution.py:23
  176.0 1.4 convert_element_type.62
  177.4 4.0 %fusion.1 = (f32[86,8192]{1,0:T(8,128)}, f32[86,8192]{1,0:T(8,128)}) fusion(s32[]{:T(128)S(6)} %select_n.22, f32[64,8192]{1,0:T(8,128)S(1)} %get-tuple-element.21, f32[64,8192]{1,0:T(8,128)S(1)} %convert_element_type.62, f32[86]{0:T(128)S(1)} %pad_dynamic-slice_fusion.6, f32[64,8192]{1,0:T(8,128)S(1)} %convert_element_type.60, f32[64,8192]{1,0:T(8,128)S(1)} %copy-done.3), kind=kLoop, calls=%fused_computation.9 | loop fusion | flops 2818048 | bytes 14025052 | tf_op jit(solution)/shard_map/concatenate | solution.py:62
  181.3 6.7 %broadcast_in_dim.14 = f32[1,86,8192]{2,0,1:T(1,128)} reshape(f32[86,8192]{1,0:T(8,128)} %get-tuple-element.30) | data formatting | bytes 5636096 | tf_op jit(solution)/shard_map/broadcast_in_dim | solution.py:63
  188.0 4.7 %broadcast_in_dim.15 = f32[1,86,8192]{2,0,1:T(1,128)} reshape(f32[86,8192]{1,0:T(8,128)S(1)} %copy-done.5) | data formatting | bytes 5636096 | tf_op jit(solution)/shard_map/broadcast_in_dim | solution.py:63
  192.8 4.1 %collective-permute-done.3 = bf16[64,8192]{1,0:T(8,128)(2,1)} collective-permute-done((bf16[64,8192]{1,0:T(8,128)(2,1)}, bf16[64,8192]{1,0:T(8,128)(2,1)}, u32[]{:S(2)}, u32[]{:S(2)}) %collective-permute-start.3) | collective-permute-done | bytes 1048608 | tf_op jit(solution)/shard_map/ppermute | solution.py:23
  196.9 3.4 %fusion.10 = bf16[1,86,8192]{2,1,0:T(8,128)(2,1)} fusion(s32[]{:T(128)S(6)} %select_n.22, bf16[64,8192]{1,0:T(8,128)(2,1)} %copy-done.6, bf16[64,8192]{1,0:T(8,128)(2,1)} %collective-permute-done.3, bf16[86]{0:T(256)(128)(2,1)S(1)} %pad_dynamic-slice_fusion.7), kind=kLoop, calls=%fused_computation.22 | loop fusion | flops 4227072 | bytes 3506352 | tf_op jit(solution)/shard_map/broadcast_in_dim | solution.py:63
  200.3 25.5 %all-gather.3.cloned.1.call-done = bf16[8,256,1024]{2,0,1:T(8,128)(2,1)} async-done(((bf16[8,64,1024]{2,0,1:T(8,128)(2,1)}), bf16[8,256,1024]{2,0,1:T(8,128)(2,1)}) %all-gather.3.cloned.1.call-update) | async-done | bytes 4194320 | tf_op jit(solution)/shard_map/all_gather | solution.py:55
  225.8 6.5 %copy.17 = bf16[8,256,1024]{2,1,0:T(8,128)(2,1)} copy(bf16[8,256,1024]{2,0,1:T(8,128)(2,1)} %all-gather.3.cloned.1.call-done) | data formatting | bytes 8388608 | tf_op jit(solution)/shard_map/all_gather | solution.py:55
  232.3 42.9 %all-gather.5.cloned.1.call-done = bf16[1024,2048]{1,0:T(8,128)(2,1)} async-done(((bf16[1024,256]{1,0:T(8,128)(2,1)}), bf16[1024,2048]{1,0:T(8,128)(2,1)}) %all-gather.5.cloned.1.call-update) | async-done | bytes 4194320 | tf_op jit(solution)/shard_map/all_gather | solution.py:33
  275.2 8.3 %convert_bitcast_fusion = bf16[1024,1024]{0,1:T(8,128)(2,1)S(1)} fusion(bf16[2048,1024]{1,0:T(8,128)(2,1)} %bitcast.44, bf16[1024,2048]{1,0:T(8,128)(2,1)} %all-gather.5.cloned.1.call-done), kind=kOutput, calls=%fused_computation.19 | convolution fusion | flops 4296015872 | bytes 10485760 | tf_op jit(solution)/shard_map/dot_general | solution.py:66
  283.5 2.6 copy.18
  286.0 0.0 copy-done.1
  (10 shorter events, 0.0 us)
Async XLA Ops:
  7.2 1.1 copy-start
  7.2 218.6 %all-gather.3.cloned.1.call-start = ((), (), s32[]{:S(2)}) async-start(), calls=%async_computation.1 | async-start | bytes 5242880 | tf_op jit(solution)/shard_map/all_gather | solution.py:55
  19.0 2.9 %copy-start.4 = (bf16[256,8192]{1,0:T(8,128)(2,1)}, bf16[256,8192]{1,0:T(8,128)(2,1)S(1)}, u32[]{:S(2)}) copy-start(bf16[256,8192]{1,0:T(8,128)(2,1)S(1)} %convolution_convert_fusion) | copy-start | bytes 12582916
  21.9 27.1 %collective-permute-start = (bf16[64,8192]{1,0:T(8,128)(2,1)}, bf16[64,8192]{1,0:T(8,128)(2,1)S(1)}, u32[]{:S(2)}, u32[]{:S(2)}) collective-permute-start(bf16[64,8192]{1,0:T(8,128)(2,1)} %get-tuple-element.26), channel_id=1, source_target_pairs={{0,8},{8,0},{16,24},{24,16},{1,9},{9,1},{17,25},{25,17},{2,10},{10... | collective-permute-start | bytes 3145736 | tf_op jit(solution)/shard_map/ppermute | solution.py:13
  24.8 47.3 %collective-permute-start.1 = (bf16[64,8192]{1,0:T(8,128)(2,1)}, bf16[64,8192]{1,0:T(8,128)(2,1)S(1)}, u32[]{:S(2)}, u32[]{:S(2)}) collective-permute-start(bf16[64,8192]{1,0:T(8,128)(2,1)} %get-tuple-element.28), channel_id=1, source_target_pairs={{0,16},{8,24},{16,0},{24,8},{1,17},{9,25},{17,1},{25,9},{2,18},{10... | collective-permute-start | bytes 3145736 | tf_op jit(solution)/shard_map/ppermute | solution.py:13
  26.4 46.8 %collective-permute-start.2 = (bf16[64,8192]{1,0:T(8,128)(2,1)}, bf16[64,8192]{1,0:T(8,128)(2,1)}, u32[]{:S(2)}, u32[]{:S(2)}) collective-permute-start(bf16[64,8192]{1,0:T(8,128)(2,1)} %get-tuple-element.27), channel_id=1, source_target_pairs={{0,24},{8,16},{16,8},{24,0},{1,25},{9,17},{17,9},{25,1},{2,26},{10... | collective-permute-start | bytes 3145736 | tf_op jit(solution)/shard_map/ppermute | solution.py:13
  27.1 51.9 %copy-start.9 = (bf16[1,64,8192]{2,1,0:T(8,128)(2,1)S(1)}, bf16[1,64,8192]{2,1,0:T(8,128)(2,1)}, u32[]{:S(2)}) copy-start(bf16[1,64,8192]{2,1,0:T(8,128)(2,1)} %param.9) | copy-start | bytes 3145732
  49.0 23.1 %copy-start.7 = (bf16[64,8192]{1,0:T(8,128)(2,1)}, bf16[64,8192]{1,0:T(8,128)(2,1)S(1)}, u32[]{:S(2)}) copy-start(bf16[64,8192]{1,0:T(8,128)(2,1)S(1)} %collective-permute-done) | copy-start | bytes 3145732
  72.2 1.0 copy-start.8
  79.0 1.3 copy-start.2
  80.3 31.4 %copy-start.6 = (bf16[64,8192]{1,0:T(8,128)(2,1)}, bf16[64,8192]{1,0:T(8,128)(2,1)S(1)}, u32[]{:S(2)}) copy-start(bf16[64,8192]{1,0:T(8,128)(2,1)S(1)} %fusion.7) | copy-start | bytes 3145732
  113.2 162.0 %all-gather.5.cloned.1.call-start = ((), (), s32[]{:S(2)}) async-start(), calls=%async_computation.2 | async-start | bytes 4718592 | tf_op jit(solution)/shard_map/all_gather | solution.py:33
  114.0 39.5 %collective-permute-start.4 = (bf16[64,8192]{1,0:T(8,128)(2,1)}, bf16[64,8192]{1,0:T(8,128)(2,1)}, u32[]{:S(2)}, u32[]{:S(2)}) collective-permute-start(bf16[64,8192]{1,0:T(8,128)(2,1)} %get-tuple-element.24), channel_id=1, source_target_pairs={{8,0},{16,8},{24,16},{9,1},{17,9},{25,17},{10,2},{18,10},{26,18},{... | collective-permute-start | bytes 3145736 | tf_op jit(solution)/shard_map/ppermute | solution.py:23
  115.3 60.7 %collective-permute-start.5 = (bf16[64,8192]{1,0:T(8,128)(2,1)}, bf16[64,8192]{1,0:T(8,128)(2,1)}, u32[]{:S(2)}, u32[]{:S(2)}) collective-permute-start(bf16[64,8192]{1,0:T(8,128)(2,1)} %get-tuple-element.20), channel_id=1, source_target_pairs={{8,0},{16,8},{24,16},{9,1},{17,9},{25,17},{10,2},{18,10},{26,18},{... | collective-permute-start | bytes 3145736 | tf_op jit(solution)/shard_map/ppermute | solution.py:23
  116.8 80.1 %collective-permute-start.3 = (bf16[64,8192]{1,0:T(8,128)(2,1)}, bf16[64,8192]{1,0:T(8,128)(2,1)}, u32[]{:S(2)}, u32[]{:S(2)}) collective-permute-start(bf16[64,8192]{1,0:T(8,128)(2,1)} %copy-done.6), channel_id=1, source_target_pairs={{8,0},{16,8},{24,16},{9,1},{17,9},{25,17},{10,2},{18,10},{26,18},{... | collective-permute-start | bytes 3145736 | tf_op jit(solution)/shard_map/ppermute | solution.py:23
  154.9 22.5 %copy-start.3 = (f32[64,8192]{1,0:T(8,128)S(1)}, f32[64,8192]{1,0:T(8,128)}, u32[]{:S(2)}) copy-start(f32[64,8192]{1,0:T(8,128)} %copy-done.2) | copy-start | bytes 6291460
  181.3 6.7 %copy-start.5 = (f32[86,8192]{1,0:T(8,128)S(1)}, f32[86,8192]{1,0:T(8,128)}, u32[]{:S(2)}) copy-start(f32[86,8192]{1,0:T(8,128)} %get-tuple-element.29) | copy-start | bytes 8454148
  275.2 10.9 %copy-start.1 = (bf16[1024,256]{1,0:T(8,128)(2,1)S(1)}, bf16[1024,256]{1,0:T(8,128)(2,1)}, u32[]{:S(2)}) copy-start(bf16[1024,256]{1,0:T(8,128)(2,1)} %param.7) | copy-start | bytes 1572868
Sparse Core Ops, SparseCore 0:
  113.3 112.3 all-gather.2
  227.4 47.7 all-gather.4

commit v2 on v1

v2 whole, which is shorter than its diff:
```python
import functools

import jax
import jax.numpy as jnp
from jax import lax
from jax.experimental import pallas as pl
from jax.experimental.pallas import tpu as pltpu
from jax.sharding import PartitionSpec as P

MESH = pl.DeviceIdType.MESH
MIB = 1 << 20


def flip(i, k):
    for bit in (1, 2, 4, 8, 16):
        if k & bit:
            i = i + bit * (1 - 2 * ((i // bit) % 2))
    return i


def kernel(
    owners, heads,
    fix, act, og, ow, om, ov, nin,
    new_w, nxt_w, new_m, nxt_m, new_v, nxt_v, out,
    og_buf, part, own, recv, ow_buf, om_buf, ov_buf, w_buf, m_buf, v_buf, m_half, v_half,
    w_cols, in_buf, acc,
    og_sem, old_sem, new_sem, rs_send, rs_recv, a2a_send, a2a_recv, ag_send, ag_recv,
    sh_send, sh_recv, in_send, in_recv, fw_send, fw_recv,
):
    d = lax.axis_index("dp")
    q = lax.axis_index("mp")
    rows = ow.shape[0]
    ws = ow.shape[1] // heads
    tokens = act.shape[0]
    half = heads // 2
    sib = flip(q, 1)

    def remote(src, dst, send, arrive, where):
        return pltpu.make_async_remote_copy(
            src_ref=src, dst_ref=dst, send_sem=send, recv_sem=arrive,
            device_id=where, device_id_type=MESH,
        )

    def cols(s):
        return pl.ds(pl.multiple_of(lax.rem(q + s, heads) * ws, ws), ws)

    def fetch(s):
        return pltpu.make_async_copy(og.at[:, cols(s)], og_buf.at[s % 2], og_sem.at[s % 2])

    def reduce_copy(s, k):
        peer = flip(d, k)
        return remote(part.at[s, peer], recv.at[s, k - 1], rs_send.at[s, k - 1],
                      rs_recv.at[s, k - 1], {"dp": peer})

    def head_copy(s):
        return remote(w_buf.at[:, cols(s)], w_cols.at[q, d], a2a_send.at[s], a2a_recv.at[s],
                      {"mp": lax.rem(q + s, heads)})

    def gather_copy(s, k):
        block = w_cols.at[lax.rem(q - s + heads, heads), d]
        return remote(block, block, ag_send.at[s, k - 1], ag_recv.at[s, k - 1],
                      {"dp": flip(d, k)})

    def shift_copies(s):
        pairs = ((w_buf.at[:, cols(s)], nxt_w), (m_half.at[s], nxt_m), (v_half.at[s], nxt_v))
        return [
            remote(src, dst.at[:, cols(s)], sh_send.at[s, j], sh_recv.at[s, j], {"dp": d - 1})
            for j, (src, dst) in enumerate(pairs)
        ]

    def input_copy(j):
        return remote(nin, in_buf.at[q], in_send.at[j], in_recv.at[j],
                      {"mp": lax.rem(q + 2 * j, heads)})

    def sibling_copy(j):
        b = lax.rem(q - 2 * j + heads, heads)
        return remote(nin if j == 0 else in_buf.at[b], in_buf.at[b], fw_send.at[j],
                      fw_recv.at[j], {"mp": sib})

    olds = [
        pltpu.make_async_copy(src, dst, old_sem.at[j])
        for j, (src, dst) in enumerate(
            ((ow, ow_buf), (om, om_buf), (ov, ov_buf), (nin, in_buf.at[q]))
        )
    ]
    fetch(0).start()
    for copy in olds:
        copy.start()

    barrier = pltpu.get_barrier_semaphore()
    for k in range(1, owners):
        pl.semaphore_signal(barrier, inc=1, device_id={"dp": flip(d, k)}, device_id_type=MESH)
    for k in range(1, heads):
        pl.semaphore_signal(
            barrier, inc=1, device_id={"mp": lax.rem(q + k, heads)}, device_id_type=MESH
        )
    pl.semaphore_wait(barrier, owners + heads - 2)

    def grad_step(s, carry):
        @pl.when(s + 1 < heads)
        def _():
            fetch(s + 1).start()

        fetch(s).wait()
        g = lax.dot_general(
            act[...], og_buf[s % 2], (((0,), (0,)), ((), ())),
            preferred_element_type=jnp.float32,
        )
        for o in range(owners):
            piece = g[o * rows:(o + 1) * rows]
            part[s, o] = piece.astype(jnp.bfloat16)

            @pl.when(d == o)
            def _():
                own[s] = piece

        for k in range(1, owners):
            reduce_copy(s, k).start()
        return carry

    lax.fori_loop(0, heads, grad_step, 0)
    for j in range(1, half):
        input_copy(j).start()
    sibling_copy(0).start()
    acc[...] = jnp.zeros_like(acc)
    for copy in olds:
        copy.wait()

    def forward(s):
        @pl.when(s > 0)
        def _():
            head_copy(s).wait_recv()

        for k in range(1, owners):
            gather_copy(s, k).start()

    def adam_step(s, carry):
        c = cols(s)
        g = own[s]
        for k in range(1, owners):
            reduce_copy(s, k).wait_recv()
            g = g + recv[s, k - 1].astype(jnp.float32)
        m = 0.9 * om_buf[:, c] + 0.1 * g
        v = 0.95 * ov_buf[:, c] + 0.05 * g * g
        update = m * fix[0] / (jnp.sqrt(v * fix[1]) + 1e-08)
        w = (ow_buf[:, c].astype(jnp.float32) - 0.01 * update).astype(jnp.bfloat16)
        m_buf[:, c] = m
        v_buf[:, c] = v
        w_buf[:, c] = w
        m_half[s] = m.astype(jnp.bfloat16)
        v_half[s] = v.astype(jnp.bfloat16)

        @pl.when(s == 0)
        def _():
            w_cols[q, d] = w

        @pl.when(s > 0)
        def _():
            head_copy(s).start()
            forward(s - 1)

        @pl.when(d > 0)
        def _():
            for copy in shift_copies(s):
                copy.start()

        return carry

    lax.fori_loop(0, heads, adam_step, 0)
    forward(heads - 1)
    news = [
        pltpu.make_async_copy(src, dst, new_sem.at[j])
        for j, (src, dst) in enumerate(((w_buf, new_w), (m_buf, new_m), (v_buf, new_v)))
    ]
    for copy in news:
        copy.start()
    for j in range(1, half):
        input_copy(j).wait_recv()
        sibling_copy(j).start()
    for j in range(half):
        sibling_copy(j).wait_recv()

    tile = min(256, tokens)

    def output_step(s, carry):
        p = lax.rem(q - s + heads, heads)
        for k in range(1, owners):
            gather_copy(s, k).wait_recv()
        w = w_cols[p].reshape(owners * rows, ws)

        def rows_step(r, inner):
            at = pl.ds(pl.multiple_of(r * tile, tile), tile)
            acc[at, :] += jnp.dot(in_buf[p, at, :], w, preferred_element_type=jnp.float32)
            return inner

        return lax.fori_loop(0, tokens // tile, rows_step, carry)

    lax.fori_loop(0, heads, output_step, 0)
    out[...] = acc[...].astype(jnp.bfloat16)

    for copy in news:
        copy.wait()
    for j in range(1, half):
        input_copy(j).wait_send()
    for j in range(half):
        sibling_copy(j).wait_send()

    def drain(s, carry):
        for k in range(1, owners):
            reduce_copy(s, k).wait_send()
            gather_copy(s, k).wait_send()

        @pl.when(s > 0)
        def _():
            head_copy(s).wait_send()

        @pl.when(d > 0)
        def _():
            for copy in shift_copies(s):
                copy.wait_send()

        @pl.when(d < owners - 1)
        def _():
            for copy in shift_copies(s):
                copy.wait_recv()

        return carry

    lax.fori_loop(0, heads, drain, 0)


def body(activations, out_grad, old_weight, old_first, old_second, step, next_input):
    owners = lax.axis_size("dp")
    heads = lax.axis_size("mp")
    owner = lax.axis_index("dp")
    _, rows, width = old_weight.shape
    tokens, part_rows = activations.shape
    held_rows = rows * owners
    shard_rows = (held_rows + owners - 2) // (owners - 1)
    ws = width // heads
    step_float = step[0].astype(jnp.float32)
    first_fix = 1.0 - jnp.power(jnp.float32(0.9), step_float)
    second_fix = 1.0 - jnp.power(jnp.float32(0.95), step_float)
    fix = jnp.stack([1.0 / first_fix, 1.0 / second_fix])

    bf16, f32 = jnp.bfloat16, jnp.float32
    full = jax.ShapeDtypeStruct((rows, width), bf16)
    wide = jax.ShapeDtypeStruct((rows, width), f32)
    anywhere = pl.BlockSpec(memory_space=pl.ANY)
    vmem = pl.BlockSpec(memory_space=pltpu.VMEM)
    dma = pltpu.SemaphoreType.DMA
    half = heads // 2
    new_w, nxt_w, new_m, nxt_m, new_v, nxt_v, output = pl.pallas_call(
        functools.partial(kernel, owners, heads),
        out_shape=(full, full, wide, full, wide, full, jax.ShapeDtypeStruct((tokens, ws), bf16)),
        in_specs=[pl.BlockSpec(memory_space=pltpu.SMEM), vmem] + [anywhere] * 5,
        out_specs=(anywhere,) * 6 + (vmem,),
        scratch_shapes=[
            pltpu.VMEM((2, tokens, ws), bf16),
            pltpu.VMEM((heads, owners, rows, ws), bf16),
            pltpu.VMEM((heads, rows, ws), f32),
            pltpu.VMEM((heads, owners - 1, rows, ws), bf16),
            pltpu.VMEM((rows, width), bf16),
            pltpu.VMEM((rows, width), f32),
            pltpu.VMEM((rows, width), f32),
            pltpu.VMEM((rows, width), bf16),
            pltpu.VMEM((rows, width), f32),
            pltpu.VMEM((rows, width), f32),
            pltpu.VMEM((heads, rows, ws), bf16),
            pltpu.VMEM((heads, rows, ws), bf16),
            pltpu.VMEM((heads, owners, rows, ws), bf16),
            pltpu.VMEM((heads, tokens, part_rows), bf16),
            pltpu.VMEM((tokens, ws), f32),
            dma((2,)), dma((4,)), dma((3,)),
            dma((heads, owners - 1)), dma((heads, owners - 1)),
            dma((heads,)), dma((heads,)),
            dma((heads, owners - 1)), dma((heads, owners - 1)),
            dma((heads, 3)), dma((heads, 3)),
            dma((half,)), dma((half,)), dma((half,)), dma((half,)),
        ],
        compiler_params=pltpu.CompilerParams(
            collective_id=0, has_side_effects=True, vmem_limit_bytes=56 * MIB
        ),
    )(fix, activations, out_grad, old_weight[0], old_first[0], old_second[0], next_input)

    begin = owner * (shard_rows - rows)

    def mine(block, behind):
        behind = jnp.where(owner == owners - 1, 0, behind.astype(block.dtype))
        both = jnp.concatenate([block, behind, jnp.zeros((shard_rows, width), block.dtype)], 0)
        return lax.dynamic_slice_in_dim(both, begin, shard_rows, 0)[None]

    return (mine(new_w, nxt_w), mine(new_m, nxt_m), mine(new_v, nxt_v), output)


def solution(mesh):
    return jax.shard_map(
        body,
        mesh=mesh,
        in_specs=(
            P("dp", "mp"),
            P("dp", None),
            P("mp", "dp", None),
            P("mp", "dp", None),
            P("mp", "dp", None),
            P(),
            P("dp", "mp"),
        ),
        out_specs=(P("mp", "dp", None), P("mp", "dp", None), P("mp", "dp", None), P("dp", "mp")),
        check_vma=False,
    )
```

time: 293 us -> 198 us (0.68)
  waiting for transfers between devices: 175 us -> 0 us
  Pallas kernels: 0 us -> 173 us
  blocking collectives: 31.3 us -> 0 us
  matrix products: 19 us -> 0 us
  between operations: 14.9 us -> 1.5 us
  local copies, waits for them, and re-layouts: 27.4 us -> 16.4 us
  other arithmetic: 17 us -> 7.5 us
  starting transfers between devices: 8.58 us -> 0 us
    pallas_call x0 -> x1, Pallas kernels: none -> 173 us  [body(): pl.pallas_call(functools.partial(kernel, owners, heads), out_shape=(full,...]
    ppermute x6 -> x0, waiting for transfers between devices: 106 us -> none  [the longest x3 60.5 us: to_front(): return lax.ppermute(block, axis, [(i, i - 1) for i in range(1, n)])]
    all_gather x2 -> x0, waiting for transfers between devices: 68.4 us -> none  [the longest x1 42.9 us: body(): input_all = lax.all_gather(next_input, 'mp', axis=1, tiled=True)]
    all_to_all x1 -> x0, blocking collectives: 31.3 us -> none  [body(): lax.all_to_all(new_weight, 'mp', split_axis=1, concat_axis=0, tiled=True)]
    dot_general x2 -> x0, matrix products: 19 us -> none  [the longest x1 10.7 us: body(): lax.dot_general(activations, out_grad, (((0,), (0,)), ((), ())), preferre...]
    convert_element_type x4 -> x0, other arithmetic: 9.64 us -> none  [the longest x3 8.57 us: mine(): behind = to_front(block.astype(jnp.bfloat16), 'dp').astype(block.dtype)]
    ppermute x6 -> x0, starting transfers between devices: 8.5 us -> none  [the longest x3 4.46 us: exchange(): return lax.ppermute(block, axis, [(i, partner(i, k, n)) for i in range(n)])]
    all_gather x1 -> x0, local copies, waits for them, and re-layouts: 6.49 us -> none  [body(): weight_cols = lax.all_gather(weight_part, 'dp', axis=1, tiled=True)]
  transfers between devices with their start and end apart: 8 -> 0, of which waited for: 7 -> 0; matrix products, arithmetic and copies ran while one was open for 10% -> 0% of each run, Pallas kernels for 0% -> 0%
where the time goes in v2:
time: 198 us
  Pallas kernels  173 us (87%)
  local copies, waits for them, and re-layouts  16.4 us (8%)
  other arithmetic  7.5 us (4%)
    pallas_call x1, Pallas kernels, body(): pl.pallas_call(functools.partial(kernel, owners, heads), out_shape=(full,...  173 us
    broadcast_in_dim x2, local copies, waits for them, and re-layouts, mine(): return lax.dynamic_slice_in_dim(both, begin, shard_rows, 0)[None]  11.3 us
    unnamed x11, local copies, waits for them, and re-layouts  4.93 us

profile of v2, /device:TPU:0, one launch (start us, length us, event | category | flops | bytes accessed | tf_op | source)
XLA Modules:
  0.0 198.1 jit_solution(15425707881021360978)
XLA Ops:
  1.4 0.6 pad_maximum_fusion.fix
  2.0 0.1 pad_dynamic-slice_fusion.7
  2.1 0.1 pad_dynamic-slice_fusion.6
  2.2 172.7 %shard_map.102 = (bf16[64,8192]{1,0:T(8,128)(2,1)}, bf16[64,8192]{1,0:T(8,128)(2,1)}, f32[64,8192]{1,0:T(8,128)}, bf16[64,8192]{1,0:T(8,128)(2,1)}, f32[64,8192]...) custom-call(f32[2]{0:T(128)} %pad_maximum_fusion.fix, bf16[1024,256]{1,0:T(8,128)(2,1)} %act.1, ...), custom_call_target="tpu_custom_call" | custom-call | tf_op jit(solution)/shard_map/pallas_call | solution.py:253
  174.9 0.0 copy-start.4
  174.9 0.0 copy-start.2
  174.9 0.0 copy-start.3
  175.0 1.5 broadcast_select_fusion
  176.4 0.1 copy-done.4
  176.5 2.0 %fusion.6 = bf16[1,86,8192]{2,1,0:T(8,128)(2,1)} fusion(s32[]{:T(128)S(6)} %select_n.25, bf16[64,8192]{1,0:T(8,128)(2,1)S(1)} %copy-done.4, bf16[64,8192]{1,0:T(8,128)(2,1)S(1)} %broadcast_select_fusion, bf16[86]{0:T(256)(128)(2,1)S(1)} %pad_dynamic-slice_fusion.7), kind=kLoop, calls=%fused_computation.14 | loop fusion | flops 4227072 | bytes 3506352 | tf_op jit(solution)/shard_map/broadcast_in_dim | solution.py:291
  178.5 0.0 copy-done.2
  178.5 0.0 copy-done.3
  178.5 0.0 copy-start
  178.5 0.0 copy-start.1
  178.5 0.4 convert_select_fusion
  178.9 1.2 copy-done
  180.1 0.6 copy-done.1
  180.7 3.0 %fusion.1 = (f32[86,8192]{1,0:T(8,128)}, f32[86,8192]{1,0:T(8,128)S(1)}) fusion(s32[]{:T(128)S(6)} %select_n.25, f32[64,8192]{1,0:T(8,128)S(1)} %copy-done.1, f32[64,8192]{1,0:T(8,128)S(1)} %get-tuple-element.20, f32[86]{0:T(128)S(1)} %pad_dynamic-slice_fusion.6, f32[64,8192]{1,0:T(8,128)S(1)} %get-tuple-element.21, f32[64,8192]{1,0:T(8,128)S(1)} %copy-done), kind=kLoop, calls=%fused_computation.7 | loop fusion | flops 2818048 | bytes 14025052 | tf_op jit(solution)/shard_map/concatenate | solution.py:290
  183.7 6.5 %broadcast_in_dim.26 = f32[1,86,8192]{2,0,1:T(1,128)} reshape(f32[86,8192]{1,0:T(8,128)} %get-tuple-element.18) | data formatting | bytes 5636096 | tf_op jit(solution)/shard_map/broadcast_in_dim | solution.py:291
  190.3 4.7 %broadcast_in_dim.25 = f32[1,86,8192]{2,0,1:T(1,128)} reshape(f32[86,8192]{1,0:T(8,128)S(1)} %get-tuple-element.19) | data formatting | bytes 5636096 | tf_op jit(solution)/shard_map/broadcast_in_dim | solution.py:291
  195.0 3.1 %copy.13 = bf16[1024,1024]{1,0:T(8,128)(2,1)} copy(bf16[1024,1024]{1,0:T(8,128)(2,1)} %get-tuple-element.29) | data formatting | bytes 4194304
  (2 shorter events, 0.0 us)
Async XLA Ops:
  174.9 1.5 copy-start.4
  174.9 3.6 %copy-start.2 = (bf16[64,8192]{1,0:T(8,128)(2,1)S(1)}, bf16[64,8192]{1,0:T(8,128)(2,1)}, u32[]{:S(2)}) copy-start(bf16[64,8192]{1,0:T(8,128)(2,1)} %get-tuple-element.14) | copy-start | bytes 3145732
  174.9 3.6 %copy-start.3 = (bf16[64,8192]{1,0:T(8,128)(2,1)S(1)}, bf16[64,8192]{1,0:T(8,128)(2,1)}, u32[]{:S(2)}) copy-start(bf16[64,8192]{1,0:T(8,128)(2,1)} %get-tuple-element.16) | copy-start | bytes 3145732
  178.5 1.6 copy-start
  178.5 2.2 %copy-start.1 = (f32[64,8192]{1,0:T(8,128)S(1)}, f32[64,8192]{1,0:T(8,128)}, u32[]{:S(2)}) copy-start(f32[64,8192]{1,0:T(8,128)} %get-tuple-element.15) | copy-start | bytes 6291460

commit v3 on v2

--- a/solution.py
+++ b/solution.py
@@ -25,7 +25,7 @@
     og_buf, part, own, recv, ow_buf, om_buf, ov_buf, w_buf, m_buf, v_buf, m_half, v_half,
     w_cols, in_buf, acc,
     og_sem, old_sem, new_sem, rs_send, rs_recv, a2a_send, a2a_recv, ag_send, ag_recv,
-    sh_send, sh_recv, in_send, in_recv, fw_send, fw_recv,
+    sh_send, sh_recv, back_send, back_recv, in_send, in_recv, fw_send, fw_recv,
 ):
     d = lax.axis_index("dp")
     q = lax.axis_index("mp")
@@ -62,11 +62,23 @@
                       {"dp": flip(d, k)})
 
     def shift_copies(s):
-        pairs = ((w_buf.at[:, cols(s)], nxt_w), (m_half.at[s], nxt_m), (v_half.at[s], nxt_v))
+        pairs = ((m_half.at[s], nxt_m), (v_half.at[s], nxt_v))
         return [
             remote(src, dst.at[:, cols(s)], sh_send.at[s, j], sh_recv.at[s, j], {"dp": d - 1})
             for j, (src, dst) in enumerate(pairs)
         ]
+
+    behind = lax.rem(d + 1, owners)
+
+    def back_own():
+        return pltpu.make_async_copy(
+            w_cols.at[q, behind], nxt_w.at[:, cols(0)], back_send.at[0]
+        )
+
+    def back_copy(s):
+        p = lax.rem(q - s + heads, heads)
+        return remote(w_cols.at[p, behind], nxt_w.at[:, cols(0)], back_send.at[s],
+                      back_recv.at[s], {"mp": p})
 
     def input_copy(j):
         return remote(nin, in_buf.at[q], in_send.at[j], in_recv.at[j],
@@ -186,6 +198,15 @@
         p = lax.rem(q - s + heads, heads)
         for k in range(1, owners):
             gather_copy(s, k).wait_recv()
+
+        @pl.when(jnp.logical_and(d < owners - 1, s == 0))
+        def _():
+            back_own().start()
+
+        @pl.when(jnp.logical_and(d < owners - 1, s > 0))
+        def _():
+            back_copy(s).start()
+
         w = w_cols[p].reshape(owners * rows, ws)
 
         def rows_step(r, inner):
@@ -223,6 +244,16 @@
         def _():
             for copy in shift_copies(s):
                 copy.wait_recv()
+
+            @pl.when(s == 0)
+            def _():
+                back_own().wait()
+
+            @pl.when(s > 0)
+            def _():
+                back_copy(s).wait_send()
+                remote(w_cols.at[q, behind], nxt_w.at[:, cols(s)], back_send.at[s],
+                       back_recv.at[s], {"mp": lax.rem(q + s, heads)}).wait_recv()
 
         return carry
 
@@ -275,7 +306,7 @@
             dma((heads, owners - 1)), dma((heads, owners - 1)),
             dma((heads,)), dma((heads,)),
             dma((heads, owners - 1)), dma((heads, owners - 1)),
-            dma((heads, 3)), dma((heads, 3)),
+            dma((heads, 2)), dma((heads, 2)), dma((heads,)), dma((heads,)),
             dma((half,)), dma((half,)), dma((half,)), dma((half,)),
         ],
         compiler_params=pltpu.CompilerParams(

time: 198 us -> 179 us (0.904)
  Pallas kernels: 173 us -> 153 us
    pallas_call x1, Pallas kernels: 173 us -> 153 us  [body(): pl.pallas_call(functools.partial(kernel, owners, heads), out_shape=(full,...]
where the time goes in v3:
time: 179 us; the launch traced here: 178 us
  Pallas kernels  153 us (85%)
  local copies, waits for them, and re-layouts  16.4 us (9%)
  other arithmetic  7.5 us (4%)
    pallas_call x1, Pallas kernels, body(): pl.pallas_call(functools.partial(kernel, owners, heads), out_shape=(full,...  153 us
    broadcast_in_dim x2, local copies, waits for them, and re-layouts, mine(): return lax.dynamic_slice_in_dim(both, begin, shard_rows, 0)[None]  11.3 us
    unnamed x11, local copies, waits for them, and re-layouts  4.93 us

profile of v3, /device:TPU:0, one launch (start us, length us, event | category | flops | bytes accessed | tf_op | source)
XLA Modules:
  0.0 178.4 jit_solution(2716347551856410134)
XLA Ops:
  1.4 0.6 pad_maximum_fusion.fix
  2.0 0.1 pad_dynamic-slice_fusion.7
  2.1 0.1 pad_dynamic-slice_fusion.6
  2.2 153.1 %shard_map.102 = (bf16[64,8192]{1,0:T(8,128)(2,1)}, bf16[64,8192]{1,0:T(8,128)(2,1)}, f32[64,8192]{1,0:T(8,128)}, bf16[64,8192]{1,0:T(8,128)(2,1)}, f32[64,8192]...) custom-call(f32[2]{0:T(128)} %pad_maximum_fusion.fix, bf16[1024,256]{1,0:T(8,128)(2,1)} %act.1, ...), custom_call_target="tpu_custom_call" | custom-call | tf_op jit(solution)/shard_map/pallas_call | solution.py:284
  155.3 0.0 copy-start.4
  155.3 0.0 copy-start.2
  155.3 0.0 copy-start.3
  155.3 1.5 broadcast_select_fusion
  156.8 0.1 copy-done.4
  156.8 2.0 %fusion.6 = bf16[1,86,8192]{2,1,0:T(8,128)(2,1)} fusion(s32[]{:T(128)S(6)} %select_n.25, bf16[64,8192]{1,0:T(8,128)(2,1)S(1)} %copy-done.4, bf16[64,8192]{1,0:T(8,128)(2,1)S(1)} %broadcast_select_fusion, bf16[86]{0:T(256)(128)(2,1)S(1)} %pad_dynamic-slice_fusion.7), kind=kLoop, calls=%fused_computation.14 | loop fusion | flops 4227072 | bytes 3506352 | tf_op jit(solution)/shard_map/broadcast_in_dim | solution.py:322
  158.8 0.0 copy-done.2
  158.8 0.0 copy-done.3
  158.8 0.0 copy-start
  158.8 0.0 copy-start.1
  158.9 0.4 convert_select_fusion
  159.3 1.2 copy-done
  160.4 0.6 copy-done.1
  161.1 3.0 %fusion.1 = (f32[86,8192]{1,0:T(8,128)}, f32[86,8192]{1,0:T(8,128)S(1)}) fusion(s32[]{:T(128)S(6)} %select_n.25, f32[64,8192]{1,0:T(8,128)S(1)} %copy-done.1, f32[64,8192]{1,0:T(8,128)S(1)} %get-tuple-element.20, f32[86]{0:T(128)S(1)} %pad_dynamic-slice_fusion.6, f32[64,8192]{1,0:T(8,128)S(1)} %get-tuple-element.21, f32[64,8192]{1,0:T(8,128)S(1)} %copy-done), kind=kLoop, calls=%fused_computation.7 | loop fusion | flops 2818048 | bytes 14025052 | tf_op jit(solution)/shard_map/concatenate | solution.py:321
  164.1 6.5 %broadcast_in_dim.26 = f32[1,86,8192]{2,0,1:T(1,128)} reshape(f32[86,8192]{1,0:T(8,128)} %get-tuple-element.18) | data formatting | bytes 5636096 | tf_op jit(solution)/shard_map/broadcast_in_dim | solution.py:322
  170.6 4.7 %broadcast_in_dim.25 = f32[1,86,8192]{2,0,1:T(1,128)} reshape(f32[86,8192]{1,0:T(8,128)S(1)} %get-tuple-element.19) | data formatting | bytes 5636096 | tf_op jit(solution)/shard_map/broadcast_in_dim | solution.py:322
  175.4 3.1 %copy.13 = bf16[1024,1024]{1,0:T(8,128)(2,1)} copy(bf16[1024,1024]{1,0:T(8,128)(2,1)} %get-tuple-element.29) | data formatting | bytes 4194304
  (2 shorter events, 0.0 us)
Async XLA Ops:
  155.3 1.5 copy-start.4
  155.3 3.6 %copy-start.2 = (bf16[64,8192]{1,0:T(8,128)(2,1)S(1)}, bf16[64,8192]{1,0:T(8,128)(2,1)}, u32[]{:S(2)}) copy-start(bf16[64,8192]{1,0:T(8,128)(2,1)} %get-tuple-element.14) | copy-start | bytes 3145732
  155.3 3.6 %copy-start.3 = (bf16[64,8192]{1,0:T(8,128)(2,1)S(1)}, bf16[64,8192]{1,0:T(8,128)(2,1)}, u32[]{:S(2)}) copy-start(bf16[64,8192]{1,0:T(8,128)(2,1)} %get-tuple-element.16) | copy-start | bytes 3145732
  158.8 1.6 copy-start
  158.8 2.2 %copy-start.1 = (f32[64,8192]{1,0:T(8,128)S(1)}, f32[64,8192]{1,0:T(8,128)}, u32[]{:S(2)}) copy-start(f32[64,8192]{1,0:T(8,128)} %get-tuple-element.15) | copy-start | bytes 6291460

commit v4 on v3

--- a/solution.py
+++ b/solution.py
@@ -61,10 +61,13 @@
         return remote(block, block, ag_send.at[s, k - 1], ag_recv.at[s, k - 1],
                       {"dp": flip(d, k)})
 
-    def shift_copies(s):
-        pairs = ((m_half.at[s], nxt_m), (v_half.at[s], nxt_v))
+    def shift_copies(s, sender):
+        short = -(-rows // (owners - 1))
+        n = min(rows, -(-short * sender // 16) * 16)
+        top = pl.ds(0, n)
+        pairs = ((m_half.at[s, top], nxt_m), (v_half.at[s, top], nxt_v))
         return [
-            remote(src, dst.at[:, cols(s)], sh_send.at[s, j], sh_recv.at[s, j], {"dp": d - 1})
+            remote(src, dst.at[top, cols(s)], sh_send.at[s, j], sh_recv.at[s, j], {"dp": d - 1})
             for j, (src, dst) in enumerate(pairs)
         ]
 
@@ -171,10 +174,11 @@
             head_copy(s).start()
             forward(s - 1)
 
-        @pl.when(d > 0)
-        def _():
-            for copy in shift_copies(s):
-                copy.start()
+        for sender in range(1, owners):
+            @pl.when(d == sender)
+            def _():
+                for copy in shift_copies(s, sender):
+                    copy.start()
 
         return carry
 
@@ -235,16 +239,19 @@
         def _():
             head_copy(s).wait_send()
 
-        @pl.when(d > 0)
-        def _():
-            for copy in shift_copies(s):
-                copy.wait_send()
+        for sender in range(1, owners):
+            @pl.when(d == sender)
+            def _():
+                for copy in shift_copies(s, sender):
+                    copy.wait_send()
+
+            @pl.when(d == sender - 1)
+            def _():
+                for copy in shift_copies(s, sender):
+                    copy.wait_recv()
 
         @pl.when(d < owners - 1)
         def _():
-            for copy in shift_copies(s):
-                copy.wait_recv()
-
             @pl.when(s == 0)
             def _():
                 back_own().wait()

time: 179 us -> 179 us (level)
  no operation moved by 1% of the time
where the time goes in v4:
time: 179 us; the launch traced here: 178 us
  Pallas kernels  153 us (85%)
  local copies, waits for them, and re-layouts  16.4 us (9%)
  other arithmetic  7.5 us (4%)
    pallas_call x1, Pallas kernels, body(): pl.pallas_call(functools.partial(kernel, owners, heads), out_shape=(full,...  153 us
    broadcast_in_dim x2, local copies, waits for them, and re-layouts, mine(): return lax.dynamic_slice_in_dim(both, begin, shard_rows, 0)[None]  11.3 us
    unnamed x11, local copies, waits for them, and re-layouts  4.93 us

profile of v4, /device:TPU:0, one launch (start us, length us, event | category | flops | bytes accessed | tf_op | source)
XLA Modules:
  0.0 178.4 jit_solution(1916928966927310864)
XLA Ops:
  1.4 0.6 pad_maximum_fusion.fix
  2.0 0.1 pad_dynamic-slice_fusion.7
  2.1 0.1 pad_dynamic-slice_fusion.6
  2.2 153.1 %shard_map.102 = (bf16[64,8192]{1,0:T(8,128)(2,1)}, bf16[64,8192]{1,0:T(8,128)(2,1)}, f32[64,8192]{1,0:T(8,128)}, bf16[64,8192]{1,0:T(8,128)(2,1)}, f32[64,8192]...) custom-call(f32[2]{0:T(128)} %pad_maximum_fusion.fix, bf16[1024,256]{1,0:T(8,128)(2,1)} %act.1, ...), custom_call_target="tpu_custom_call" | custom-call | tf_op jit(solution)/shard_map/pallas_call | solution.py:291
  155.3 0.0 copy-start.4
  155.3 0.0 copy-start.2
  155.3 0.0 copy-start.3
  155.3 1.5 broadcast_select_fusion
  156.8 0.1 copy-done.4
  156.8 2.0 %fusion.6 = bf16[1,86,8192]{2,1,0:T(8,128)(2,1)} fusion(s32[]{:T(128)S(6)} %select_n.25, bf16[64,8192]{1,0:T(8,128)(2,1)S(1)} %copy-done.4, bf16[64,8192]{1,0:T(8,128)(2,1)S(1)} %broadcast_select_fusion, bf16[86]{0:T(256)(128)(2,1)S(1)} %pad_dynamic-slice_fusion.7), kind=kLoop, calls=%fused_computation.14 | loop fusion | flops 4227072 | bytes 3506352 | tf_op jit(solution)/shard_map/broadcast_in_dim | solution.py:329
  158.8 0.0 copy-done.2
  158.8 0.0 copy-done.3
  158.8 0.0 copy-start
  158.8 0.0 copy-start.1
  158.9 0.4 convert_select_fusion
  159.3 1.2 copy-done
  160.4 0.6 copy-done.1
  161.1 3.0 %fusion.1 = (f32[86,8192]{1,0:T(8,128)}, f32[86,8192]{1,0:T(8,128)S(1)}) fusion(s32[]{:T(128)S(6)} %select_n.25, f32[64,8192]{1,0:T(8,128)S(1)} %copy-done.1, f32[64,8192]{1,0:T(8,128)S(1)} %get-tuple-element.20, f32[86]{0:T(128)S(1)} %pad_dynamic-slice_fusion.6, f32[64,8192]{1,0:T(8,128)S(1)} %get-tuple-element.21, f32[64,8192]{1,0:T(8,128)S(1)} %copy-done), kind=kLoop, calls=%fused_computation.7 | loop fusion | flops 2818048 | bytes 14025052 | tf_op jit(solution)/shard_map/concatenate | solution.py:328
  164.1 6.5 %broadcast_in_dim.26 = f32[1,86,8192]{2,0,1:T(1,128)} reshape(f32[86,8192]{1,0:T(8,128)} %get-tuple-element.18) | data formatting | bytes 5636096 | tf_op jit(solution)/shard_map/broadcast_in_dim | solution.py:329
  170.6 4.7 %broadcast_in_dim.25 = f32[1,86,8192]{2,0,1:T(1,128)} reshape(f32[86,8192]{1,0:T(8,128)S(1)} %get-tuple-element.19) | data formatting | bytes 5636096 | tf_op jit(solution)/shard_map/broadcast_in_dim | solution.py:329
  175.4 3.1 %copy.13 = bf16[1024,1024]{1,0:T(8,128)(2,1)} copy(bf16[1024,1024]{1,0:T(8,128)(2,1)} %get-tuple-element.29) | data formatting | bytes 4194304
  (2 shorter events, 0.0 us)
Async XLA Ops:
  155.3 1.5 copy-start.4
  155.3 3.6 %copy-start.2 = (bf16[64,8192]{1,0:T(8,128)(2,1)S(1)}, bf16[64,8192]{1,0:T(8,128)(2,1)}, u32[]{:S(2)}) copy-start(bf16[64,8192]{1,0:T(8,128)(2,1)} %get-tuple-element.14) | copy-start | bytes 3145732
  155.3 3.6 %copy-start.3 = (bf16[64,8192]{1,0:T(8,128)(2,1)S(1)}, bf16[64,8192]{1,0:T(8,128)(2,1)}, u32[]{:S(2)}) copy-start(bf16[64,8192]{1,0:T(8,128)(2,1)} %get-tuple-element.16) | copy-start | bytes 3145732
  158.8 1.6 copy-start
  158.8 2.2 %copy-start.1 = (f32[64,8192]{1,0:T(8,128)S(1)}, f32[64,8192]{1,0:T(8,128)}, u32[]{:S(2)}) copy-start(f32[64,8192]{1,0:T(8,128)} %get-tuple-element.15) | copy-start | bytes 6291460
